TPU v7x, 32 devices: a whole 2x2x4 slice. The times are simulated.
32 devices in a mesh: dp: 16 (over z, y, core), tensor: 2 (over x).
Axes of the slice: x: 2, y: 2, z: 4, core: 2. Of those that a mesh axis runs over, the one named last changes fastest.
Arguments:
- images: bfloat16 [16, 577, 1024], P('dp'), may hold values from -6 to 6
- teacher: bfloat16 [16, 577, 1024], P('dp'), may hold values from -8 to 8
- image_mask: int32 [16], P('dp'), may hold values from 0 to 1, as said below
- attn_gain: bfloat16 [1024], replicated, may hold values from 0.5 to 1.5
- attn_shift: bfloat16 [1024], replicated, may hold values from -0.5 to 0.5
- in_weight: bfloat16 [1024, 3, 1024], P(None, None, 'tensor'), may hold values from -0.1875 to 0.1875
- in_bias: bfloat16 [2, 1024], P(None, 'tensor'), may hold values from -0.5 to 0.5
- out_weight: bfloat16 [1024, 1024], P('tensor'), may hold values from -2 to 2
- out_bias: bfloat16 [1024], replicated, may hold values from -1 to 1
- mlp_gain: bfloat16 [1024], replicated, may hold values from 0.5 to 1.5
- mlp_shift: bfloat16 [1024], replicated, may hold values from -1 to 1
- up_weight: bfloat16 [1024, 4096], P(None, 'tensor'), may hold values from -0.1875 to 0.1875
- up_bias: bfloat16 [4096], P('tensor'), may hold values from -4 to 4
- down_weight: bfloat16 [4096, 1024], P('tensor'), may hold values from -0.1875 to 0.1875
- down_bias: bfloat16 [1024], replicated, may hold values from -1 to 1
Outputs:
- block_out: bfloat16 [16, 577, 1024], P('dp')
- loss: float32 [], replicated
- grad_images: bfloat16 [16, 577, 1024], P('dp')
- grad_attn_gain: float32 [1024], replicated
- grad_attn_shift: float32 [1024], replicated
- grad_in_weight: float32 [1024, 3, 1024], P('dp', None, 'tensor')
- grad_in_bias: float32 [2, 1024], P(None, 'tensor')
- grad_out_weight: float32 [1024, 1024], P('tensor', 'dp')
- grad_out_bias: float32 [1024], replicated
- grad_mlp_gain: float32 [1024], replicated
- grad_mlp_shift: float32 [1024], replicated
- grad_up_weight: float32 [1024, 4096], P('dp', 'tensor')
- grad_up_bias: float32 [4096], P('tensor')
- grad_down_weight: float32 [4096, 1024], P('tensor', 'dp')
- grad_down_bias: float32 [1024], replicated
Inputs may be any that keep to these rules, and one draw needn't show every extreme that they name: `image_mask`: the first image is always a real one.
All inputs are finite; a program needn't handle non-finite values.
Results may differ from a plain program's by a relative error of at most 0.0085.
Values sent between devices are 32-bit elements; how exact they have to be, the bound alone decides.
No kernel may reach another device: no remote copies, remote signals or barrier semaphores. Data moves between devices by JAX's collectives and lax.ppermute only.
A program may use at most 128 MiB of HBM per device.

v0:
```python
import jax
import jax.numpy as jnp
from jax import lax
from jax.sharding import PartitionSpec as P

HD = 64


epsilon = 1e-05
score_scale = 0.125
quick_rate = 1.702


def layer_norm(hidden, scales, offset):
    centred = hidden - jnp.mean(hidden, axis=-1, keepdims=True)
    inverse = lax.rsqrt(jnp.mean(centred * centred, axis=-1, keepdims=True) + epsilon)
    normed = centred * inverse
    return (normed * scales + offset, normed, inverse)


def norm_back(grad_out, normed, inverse, scales):
    scaled = grad_out * scales
    centred = scaled - jnp.mean(scaled, axis=-1, keepdims=True)
    return (centred - normed * jnp.mean(scaled * normed, axis=-1, keepdims=True)) * inverse


def contract_rows(matrix_a, matrix_b):
    return lax.dot_general(
        matrix_a, matrix_b, (((0,), (0,)), ((), ())), preferred_element_type=jnp.float32
    )


def contract_cols(matrix_a, matrix_b):
    return lax.dot_general(
        matrix_a, matrix_b, (((1,), (1,)), ((), ())), preferred_element_type=jnp.float32
    )


def attend_forward(pieces):
    query_heads, key_heads, value_heads = pieces
    scores = (
        jnp.einsum("qhd,khd->hqk", query_heads, key_heads, preferred_element_type=jnp.float32)
        * score_scale
    )
    row_max = jnp.max(scores, axis=-1, keepdims=True)
    weights = jnp.exp(scores - row_max)
    row_total = jnp.sum(weights, axis=-1, keepdims=True)
    weights_low = (weights / row_total).astype(jnp.bfloat16)
    context = jnp.einsum(
        "hqk,khd->qhd", weights_low, value_heads, preferred_element_type=jnp.float32
    )
    return (context.astype(jnp.bfloat16), (row_max + jnp.log(row_total))[..., 0])


def attend_backward(pieces):
    query_heads, key_heads, value_heads, log_total, grad_context = pieces
    scores = (
        jnp.einsum("qhd,khd->hqk", query_heads, key_heads, preferred_element_type=jnp.float32)
        * score_scale
    )
    weights = jnp.exp(scores - log_total[..., None])
    weights_low = weights.astype(jnp.bfloat16)
    grad_values = jnp.einsum(
        "hqk,qhd->khd", weights_low, grad_context, preferred_element_type=jnp.float32
    )
    grad_weights = jnp.einsum(
        "qhd,khd->hqk", grad_context, value_heads, preferred_element_type=jnp.float32
    )
    grad_scores = (
        weights * (grad_weights - jnp.sum(grad_weights * weights, axis=-1, keepdims=True))
    ).astype(jnp.bfloat16)
    grad_query = (
        jnp.einsum("hqk,khd->qhd", grad_scores, key_heads, preferred_element_type=jnp.float32)
        * score_scale
    )
    grad_keys = (
        jnp.einsum("hqk,qhd->khd", grad_scores, query_heads, preferred_element_type=jnp.float32)
        * score_scale
    )
    return (
        grad_query.astype(jnp.bfloat16),
        grad_keys.astype(jnp.bfloat16),
        grad_values.astype(jnp.bfloat16),
    )


def shards(
    images,
    teacher,
    image_mask,
    attn_gain,
    attn_shift,
    in_weight,
    in_bias,
    out_weight,
    out_bias,
    mlp_gain,
    mlp_shift,
    up_weight,
    up_bias,
    down_weight,
    down_bias,
):
    image_count, seq_len, width = images.shape
    row_count = image_count * seq_len
    local_width = in_weight.shape[2]
    head_shape = (image_count, seq_len, local_width // HD, HD)
    hidden = images.reshape(row_count, width).astype(jnp.float32)
    gain_one = attn_gain.astype(jnp.float32)
    gain_two = mlp_gain.astype(jnp.float32)
    bias_in = in_bias.astype(jnp.float32)
    normed_out, normed_one, inverse_one = layer_norm(
        hidden, gain_one, attn_shift.astype(jnp.float32)
    )
    act_one = normed_out.astype(jnp.bfloat16)
    projected = jnp.dot(
        act_one, in_weight.reshape(width, 3 * local_width), preferred_element_type=jnp.float32
    ).reshape(row_count, 3, local_width)
    query_rows = (projected[:, 0] + bias_in[0]).astype(jnp.bfloat16).reshape(head_shape)
    key_rows = projected[:, 1].astype(jnp.bfloat16).reshape(head_shape)
    value_rows = (projected[:, 2] + bias_in[1]).astype(jnp.bfloat16).reshape(head_shape)
    context, log_total = lax.map(attend_forward, (query_rows, key_rows, value_rows))
    context = context.reshape(row_count, local_width)
    attn_part = jnp.dot(context, out_weight, preferred_element_type=jnp.float32)
    attn_branch = lax.psum(attn_part, "tensor")
    middle = hidden + attn_branch + out_bias.astype(jnp.float32)
    normed_out, normed_two, inverse_two = layer_norm(
        middle, gain_two, mlp_shift.astype(jnp.float32)
    )
    act_two = normed_out.astype(jnp.bfloat16)
    pre_act = jnp.dot(act_two, up_weight, preferred_element_type=jnp.float32) + up_bias.astype(
        jnp.float32
    )
    sigma = jax.nn.sigmoid(quick_rate * pre_act)
    inner = (pre_act * sigma).astype(jnp.bfloat16)
    mlp_part = jnp.dot(inner, down_weight, preferred_element_type=jnp.float32)
    mlp_branch = lax.psum(mlp_part, "tensor")
    result = middle + mlp_branch + down_bias.astype(jnp.float32)
    valid = jnp.repeat(image_mask.astype(jnp.float32), seq_len)[:, None]
    error = result - teacher.reshape(row_count, width).astype(jnp.float32)
    squares_local = jnp.sum(valid * error * error)
    count_local = jnp.sum(image_mask.astype(jnp.float32)) * seq_len
    squares_all, count_all = lax.psum((squares_local, count_local), "dp")
    loss = squares_all / count_all
    grad_result = 2.0 * valid * error / count_all
    grad_down_bias = jnp.sum(grad_result, axis=0)
    grad_low = grad_result.astype(jnp.bfloat16)
    grad_down_weight = contract_rows(inner, grad_low)
    grad_inner = contract_cols(grad_low, down_weight)
    grad_pre = (grad_inner * (sigma + pre_act * quick_rate * sigma * (1.0 - sigma))).astype(
        jnp.bfloat16
    )
    grad_up_bias = jnp.sum(grad_pre.astype(jnp.float32), axis=0)
    grad_up_weight = contract_rows(act_two, grad_pre)
    grad_two_part = contract_cols(grad_pre, up_weight)
    grad_two = lax.psum(grad_two_part, "tensor")
    grad_mlp_gain = jnp.sum(grad_two * normed_two, axis=0)
    grad_mlp_shift = jnp.sum(grad_two, axis=0)
    grad_middle = grad_result + norm_back(grad_two, normed_two, inverse_two, gain_two)
    grad_out_bias = jnp.sum(grad_middle, axis=0)
    grad_attn = grad_middle.astype(jnp.bfloat16)
    grad_out_weight = contract_rows(context, grad_attn)
    grad_context = contract_cols(grad_attn, out_weight).astype(jnp.bfloat16).reshape(head_shape)
    grad_query, grad_keys, grad_values = lax.map(
        attend_backward, (query_rows, key_rows, value_rows, log_total, grad_context)
    )
    grad_projected = jnp.stack(
        [
            grad_query.reshape(row_count, local_width),
            grad_keys.reshape(row_count, local_width),
            grad_values.reshape(row_count, local_width),
        ],
        axis=1,
    ).reshape(row_count, 3 * local_width)
    grad_in_bias = jnp.stack(
        [
            jnp.sum(grad_query.astype(jnp.float32), axis=(0, 1)).reshape(-1),
            jnp.sum(grad_values.astype(jnp.float32), axis=(0, 1)).reshape(-1),
        ]
    )
    grad_in_weight = contract_rows(act_one, grad_projected).reshape(width, 3, local_width)
    grad_one_part = contract_cols(grad_projected, in_weight.reshape(width, 3 * local_width))
    grad_one = lax.psum(grad_one_part, "tensor")
    grad_attn_gain = jnp.sum(grad_one * normed_one, axis=0)
    grad_attn_shift = jnp.sum(grad_one, axis=0)
    grad_images = (
        (grad_middle + norm_back(grad_one, normed_one, inverse_one, gain_one))
        .reshape(image_count, seq_len, width)
        .astype(jnp.bfloat16)
    )
    full_in, full_out, full_up, full_down = (
        lax.psum_scatter(grad_in_weight, "dp", scatter_dimension=0, tiled=True),
        lax.psum_scatter(grad_out_weight, "dp", scatter_dimension=1, tiled=True),
        lax.psum_scatter(grad_up_weight, "dp", scatter_dimension=0, tiled=True),
        lax.psum_scatter(grad_down_weight, "dp", scatter_dimension=1, tiled=True),
    )
    small_all = lax.psum(
        (
            grad_attn_gain,
            grad_attn_shift,
            grad_in_bias,
            grad_out_bias,
            grad_mlp_gain,
            grad_mlp_shift,
            grad_up_bias,
            grad_down_bias,
        ),
        "dp",
    )
    small_attn = small_all[:4]
    small_mlp = small_all[4:]
    block_out = result.reshape(image_count, seq_len, width).astype(jnp.bfloat16)
    return (
        block_out,
        loss,
        grad_images,
        small_attn[0],
        small_attn[1],
        full_in,
        small_attn[2],
        full_out,
        small_attn[3],
        small_mlp[0],
        small_mlp[1],
        full_up,
        small_mlp[2],
        full_down,
        small_mlp[3],
    )


def solution(mesh):
    placed = (
        P("dp", None, None),
        P("dp", None, None),
        P("dp"),
        P(),
        P(),
        P(None, None, "tensor"),
        P(None, "tensor"),
        P("tensor", None),
        P(),
        P(),
        P(),
        P(None, "tensor"),
        P("tensor"),
        P("tensor", None),
        P(),
    )
    return jax.shard_map(
        shards,
        mesh=mesh,
        in_specs=placed,
        out_specs=(
            P("dp", None, None),
            P(),
            P("dp", None, None),
            P(),
            P(),
            P("dp", None, "tensor"),
            P(None, "tensor"),
            P("tensor", "dp"),
            P(),
            P(),
            P(),
            P("dp", "tensor"),
            P("tensor"),
            P("tensor", "dp"),
            P(),
        ),
        check_vma=False,
    )
```

profile of v0, /device:TPU:0, one launch (start us, length us, event | category | flops | bytes accessed | tf_op | source)
XLA Modules:
  0.0 782.1 jit_solution(11940931965776615431)
XLA Ops:
  7.3 1.6 convert_reduce_fusion.1
  8.9 1.7 fusion.22
  10.7 4.8 copy.43
  15.5 4.2 fusion.7
  22.3 1.8 copy.46
  24.9 2.8 copy.44
  27.7 2.1 multiply_reduce_fusion.1
  29.9 2.1 fusion
  32.0 2.4 copy-done.2
  34.3 2.9 fusion.36
  38.1 2.3 fusion.61
  41.1 71.5 %all-reduce.6.cloned.1.call-done = f32[577,1024]{1,0:T(8,128)} async-done(((f32[577,1024]{1,0:T(8,128)}), f32[577,1024]{1,0:T(8,128)}) %all-reduce.6.cloned.1.call-update) | async-done | bytes 2363408 | tf_op jit(solution)/shard_map/psum | solution.py:125
  112.6 2.5 fusion.58
  115.9 2.9 fusion.54
  118.8 2.2 copy-done.40
  121.1 4.1 fusion.55
  125.9 33.7 %psum.101 = f32[]{:T(128)} all-reduce(f32[]{:T(128)S(6)} %mul.183), channel_id=1, replica_groups=mesh['dp'=16,'tensor'=2] {'dp'}, use_global_device_ids=true, to_apply=%region_10.11 | all-reduce | flops 1 | bytes 8 | tf_op jit(solution)/shard_map/psum | solution.py:143
  159.6 35.1 %all-reduce.8.cloned.1.call-done = f32[577,1024]{1,0:T(8,128)} async-done(((f32[577,1024]{1,0:T(8,128)}), f32[577,1024]{1,0:T(8,128)}) %all-reduce.8.cloned.1.call-update) | async-done | bytes 2363408 | tf_op jit(solution)/shard_map/psum | solution.py:137
  194.7 4.6 fusion.56
  199.3 7.8 convert_reduce_fusion
  207.1 1.4 copy-done.41
  208.5 4.1 fusion.62
  213.0 69.2 %all-reduce.10.cloned.1.call-done = f32[577,1024]{1,0:T(8,128)} async-done(((f32[577,1024]{1,0:T(8,128)}), f32[577,1024]{1,0:T(8,128)}) %all-reduce.10.cloned.1.call-update) | async-done | bytes 2363408 | tf_op jit(solution)/shard_map/psum | solution.py:156
  282.2 2.8 multiply_reduce_fusion.2
  285.3 4.1 fusion.57
  289.4 1.4 copy-done.3
  290.8 1.6 convolution_convert_fusion
  292.5 1.4 copy.48
  293.9 12.1 %multiply_reduce_fusion = (f32[8,577]{1,0:T(8,128)S(1)}, f32[8,577,577]{1,2,0:T(8,128)}) fusion(f32[8,577,577]{1,2,0:T(8,128)} %copy-done.2, f32[8,577]{1,0:T(8,128)S(1)} %log_add_fusion, bf16[577,8,64]{0,2,1:T(8,128)(2,1)S(1)} %bitcast.118, f32[577,8,64]{0,2,1:T(8,128)} %bitcast.120, f32[8,64]{1,0:T(8,128)S(1)} %add.151), kind=kOutput, calls=%fused_computation.1 | convolution fusion | flops 352159232 | bytes 23118976 | tf_op jit(solution)/shard_map/while/body/eval_jaxpr/qhd,khd->hqk/dot_general | solution.py:66
  306.0 6.3 multiply_convert_fusion
  312.3 2.1 convert_reduce_fusion.3
  314.4 2.7 fusion.32
  317.1 3.1 convert_reduce_fusion.2
  320.3 2.2 copy.52
  322.5 2.1 copy.53
  325.7 5.9 convolution_bitcast_fusion
  332.7 4.1 fusion.39
  336.9 7.8 fusion.29
  344.7 7.7 fusion.53
  352.5 1.7 copy-done.10
  354.1 10.2 %fusion.42 = f32[2048,1024]{0,1:T(8,128)} fusion(f32[577,2048]{1,0:T(8,128)} %copy-done.40, f32[2048]{0:T(1024)S(1)} %convert_element_type.162, f32[577,1024]{1,0:T(8,128)S(1)} %copy-done.10, bf16[1,577,1024]{2,1,0:T(8,128)(2,1)} %param.16, f32[]{:T(128)} %psum.101, f32[]{:T(128)S(6)} %mul.184), kind=kOutput, calls=%fused_computation.75 | convolution fusion | flops 2431339520 | bytes 16668680 | tf_op jit(solution)/shard_map/dot_general | solution.py:28
  364.5 36.6 %all-reduce.12.cloned.1.call-done = f32[577,1024]{1,0:T(8,128)} async-done(((f32[577,1024]{1,0:T(8,128)}), f32[577,1024]{1,0:T(8,128)}) %all-reduce.12.cloned.1.call-update) | async-done | bytes 2363408 | tf_op jit(solution)/shard_map/psum | solution.py:183
  401.1 3.0 fusion.21
  404.2 62.3 %all-reduce = (f32[]{:T(128)}, f32[1024]{0:T(1024)}, f32[1024]{0:T(1024)}, f32[2,512]{1,0:T(2,128)}, f32[1024]{0:T(1024)}, /*index=5*/f32[1024]{0:T(1024)}, f32[1024]{0:T(1024)}, f32[2048]{0:T(1024)}, f32[1024]{0:T(1024)}) all-reduce(f32[]{:T(128)} %get-tuple-element.65, ...), channel_id=1, replica_groups=mesh['dp'=16,'tensor'=2] {'dp'}, use_global_device_ids=true, to_apply=%region_9.10 | all-reduce | flops 9217 | bytes 73736 | tf_op jit(solution)/shard_map/psum | solution.py:143
  467.8 4.0 fusion.38
  471.8 84.3 %reduce-scatter.5.cloned.1.call-done = f32[64,3,512]{2,0,1:T(8,128)} async-done(((f32[1024,3,512]{2,0,1:T(8,128)}), f32[64,3,512]{2,0,1:T(8,128)}) %reduce-scatter.5.cloned.1.call-update) | async-done | bytes 393232 | tf_op jit(solution)/shard_map/reduce_scatter | solution.py:192
  556.1 108.5 %reduce-scatter.9.cloned.1.call-done = f32[64,2048]{1,0:T(8,128)} async-done(((f32[1024,2048]{1,0:T(8,128)}), f32[64,2048]{1,0:T(8,128)}) %reduce-scatter.9.cloned.1.call-update) | async-done | bytes 524304 | tf_op jit(solution)/shard_map/reduce_scatter | solution.py:194
  664.6 109.1 %reduce-scatter.11.cloned.1.call-done = f32[2048,64]{0,1:T(8,128)} async-done(((f32[2048,1024]{0,1:T(8,128)}), f32[2048,64]{0,1:T(8,128)}) %reduce-scatter.11.cloned.1.call-update) | async-done | bytes 524304 | tf_op jit(solution)/shard_map/reduce_scatter | solution.py:195
  (130 shorter events, 9.0 us)
Async XLA Ops:
  7.2 30.9 %copy-start = (bf16[512,1024]{1,0:T(8,128)(2,1)S(1)}, bf16[512,1024]{1,0:T(8,128)(2,1)}, u32[]{:S(2)}) copy-start(bf16[512,1024]{1,0:T(8,128)(2,1)} %param.22) | copy-start | bytes 3145732
  7.2 3.4 copy-start.30
  7.2 3.5 copy-start.31
  7.2 105.4 %all-reduce.6.cloned.1.call-start = ((), (), s32[]{:S(2)}) async-start(), calls=%async_computation.4 | async-start | bytes 4784128 | tf_op jit(solution)/shard_map/psum | solution.py:125
  8.9 6.6 copy-start.21
  10.6 4.9 copy-start.23
  10.7 4.8 copy-start.25
  10.7 4.8 copy-start.28
  10.7 4.8 copy-start.5
  22.3 7.6 copy-start.6
  24.1 5.8 copy-start.12
  29.9 4.4 copy-start.2
  29.9 4.4 copy-start.16
  40.4 154.3 %all-reduce.8.cloned.1.call-start = ((), (), s32[]{:S(2)}) async-start(), calls=%async_computation.5 | async-start | bytes 4784128 | tf_op jit(solution)/shard_map/psum | solution.py:137
  112.6 3.3 copy-start.38
  115.9 5.2 copy-start.36
  118.8 2.2 copy-start.40
  125.2 34.4 %copy-start.35 = (bf16[1024]{0:T(1024)(128)(2,1)S(1)}, bf16[1024]{0:T(1024)(128)(2,1)}, u32[]{:S(2)}) copy-start(bf16[1024]{0:T(1024)(128)(2,1)} %param.29) | copy-start | bytes 6148
  125.2 157.0 %all-reduce.10.cloned.1.call-start = ((), (), s32[]{:S(2)}) async-start(), calls=%async_computation.6 | async-start | bytes 4784128 | tf_op jit(solution)/shard_map/psum | solution.py:156
  194.7 4.6 copy-start.17
  194.7 4.6 copy-start.37
  199.3 7.8 copy-start.8
  199.3 9.2 %copy-start.39 = (bf16[1024,2048]{1,0:T(8,128)(2,1)S(1)}, bf16[1024,2048]{1,0:T(8,128)(2,1)}, u32[]{:S(2)}) copy-start(bf16[1024,2048]{1,0:T(8,128)(2,1)} %param.26) | copy-start | bytes 12582916
  207.1 1.4 copy-start.41
  212.7 188.4 %all-reduce.12.cloned.1.call-start = ((), (), s32[]{:S(2)}) async-start(), calls=%async_computation.7 | async-start | bytes 4784128 | tf_op jit(solution)/shard_map/psum | solution.py:183
  282.2 2.8 copy-start.9
  282.2 3.1 copy-start.11
  289.4 1.4 copy-start.3
  293.8 12.2 %copy-start.14 = (bf16[577,512]{0,1:T(8,128)(2,1)}, bf16[577,512]{0,1:T(8,128)(2,1)S(1)}, u32[]{:S(2)}) copy-start(bf16[577,512]{0,1:T(8,128)(2,1)S(1)} %copy.48) | copy-start | bytes 1772548
  293.8 12.1 %slice-start = ((s8[11960320]{0:T(1024)(128)(4,1)}), s8[4194304]{0:T(1024)(128)(4,1)S(1)}, s32[]{:S(2)}) async-start(s8[11960320]{0:T(1024)(128)(4,1)} %bitcast.112), calls=%async_computation.12 | async-start | bytes 8388608
  293.8 12.1 %slice-start.1 = ((s8[11960320]{0:T(1024)(128)(4,1)}), s8[4194304]{0:T(1024)(128)(4,1)S(1)}, s32[]{:S(2)}) async-start(s8[11960320]{0:T(1024)(128)(4,1)} %bitcast.112), calls=%async_computation.13 | async-start | bytes 8388608
  293.9 12.1 %slice-start.2 = ((s8[11960320]{0:T(1024)(128)(4,1)}), s8[3571712]{0:T(1024)(128)(4,1)S(1)}, s32[]{:S(2)}) async-start(s8[11960320]{0:T(1024)(128)(4,1)} %bitcast.112), calls=%async_computation.14 | async-start | bytes 7143424
  306.0 6.3 copy-start.13
  312.3 2.1 copy-start.7
  314.4 2.7 copy-start.15
  320.3 4.3 copy-start.20
  331.6 1.1 copy-start.19
  331.6 5.2 copy-start.22
  331.6 5.2 copy-start.24
  331.6 5.2 copy-start.26
  331.6 5.2 copy-start.29
  331.7 140.1 %reduce-scatter.7.cloned.1.call-start = ((), (), s32[]{:S(2)}) async-start(), calls=%async_computation.9 | async-start | bytes 2228224 | tf_op jit(solution)/shard_map/reduce_scatter | solution.py:193
  336.8 219.3 %reduce-scatter.5.cloned.1.call-start = ((), (), s32[]{:S(2)}) async-start(), calls=%async_computation.8 | async-start | bytes 6684672 | tf_op jit(solution)/shard_map/reduce_scatter | solution.py:192
  344.7 319.9 %reduce-scatter.9.cloned.1.call-start = ((), (), s32[]{:S(2)}) async-start(), calls=%async_computation.10 | async-start | bytes 8912896 | tf_op jit(solution)/shard_map/reduce_scatter | solution.py:194
  352.4 1.7 copy-start.10
  352.4 421.2 %reduce-scatter.11.cloned.1.call-start = ((), (), s32[]{:S(2)}) async-start(), calls=%async_computation.11 | async-start | bytes 8912896 | tf_op jit(solution)/shard_map/reduce_scatter | solution.py:195
  364.4 103.4 %copy-start.4 = (f32[577,1024]{1,0:T(8,128)S(1)}, f32[577,1024]{1,0:T(8,128)}, u32[]{:S(2)}) copy-start(f32[577,1024]{1,0:T(8,128)} %copy-done.3) | copy-start | bytes 7090180
  467.8 305.9 %copy-start.1 = (bf16[512,1024]{1,0:T(8,128)(2,1)S(1)}, bf16[512,1024]{1,0:T(8,128)(2,1)}, u32[]{:S(2)}) copy-start(bf16[512,1024]{1,0:T(8,128)(2,1)} %param.22) | copy-start | bytes 3145732
  (5 other events, 3.7 us)
Sparse Core Ops, SparseCore 0:
  40.5 72.0 all-reduce.5
  125.3 69.3 all-reduce.7
  212.8 69.3 all-reduce.9
  331.7 69.3 all-reduce.11
  405.3 61.6 reduce-scatter.6
  471.9 84.1 reduce-scatter.4
  560.7 103.7 reduce-scatter.8
  669.2 104.4 reduce-scatter.10
where the time goes:
time: 790 us; the launch traced here: 782 us
  waiting for transfers between devices  514 us (65%)
  blocking collectives  95.9 us (12%)
  matrix products  87.8 us (11%)
  other arithmetic  33.9 us (4%)
  local copies, waits for them, and re-layouts  30.8 us (4%)
  between operations  18.2 us (2%)
    reduce_scatter x1, waiting for transfers between devices, shards(): lax.psum_scatter(grad_down_weight, 'dp', scatter_dimension=1, tiled=True)  109 us
    reduce_scatter x1, waiting for transfers between devices, shards(): lax.psum_scatter(grad_up_weight, 'dp', scatter_dimension=0, tiled=True)  108 us
    psum x2, blocking collectives, shards(): squares_all, count_all = lax.psum((squares_local, count_local), 'dp')  95.9 us
    reduce_scatter x1, waiting for transfers between devices, shards(): lax.psum_scatter(grad_in_weight, 'dp', scatter_dimension=0, tiled=True)  84.3 us
    psum x1, waiting for transfers between devices, shards(): attn_branch = lax.psum(attn_part, 'tensor')  71.5 us
    psum x1, waiting for transfers between devices, shards(): grad_two = lax.psum(grad_two_part, 'tensor')  69.2 us
    psum x1, waiting for transfers between devices, shards(): grad_one = lax.psum(grad_one_part, 'tensor')  36.6 us
    psum x1, waiting for transfers between devices, shards(): mlp_branch = lax.psum(mlp_part, 'tensor')  35.1 us
  transfers between devices with their start and end apart: 8, of which 7 were waited for; matrix products, arithmetic and copies ran while one was open for 5% of the time, Pallas kernels for 0%

commit v1 on v0

v1 whole, which is shorter than its diff:
```python
import jax
import jax.numpy as jnp
from jax import lax
from jax.experimental import pallas as pl
from jax.experimental.pallas import tpu as pltpu
from jax.sharding import PartitionSpec as P

HD = 64

epsilon = 1e-05
score_scale = 0.125
quick_rate = 1.702
log2_e = 1.4426950408889634
score_rate = score_scale * log2_e

NN = (((1,), (0,)), ((), ()))
NT = (((1,), (1,)), ((), ()))
VMEM_BYTES = 48 * 2**20


def dot(matrix_a, matrix_b, dims=NN):
    return lax.dot_general(matrix_a, matrix_b, dims, preferred_element_type=jnp.float32)


def layer_norm(hidden, scales, offset):
    centred = hidden - jnp.mean(hidden, axis=-1, keepdims=True)
    inverse = lax.rsqrt(jnp.mean(centred * centred, axis=-1, keepdims=True) + epsilon)
    normed = centred * inverse
    return (normed * scales + offset, normed, inverse)


def norm_back(grad_out, normed, inverse, scales):
    scaled = grad_out * scales
    centred = scaled - jnp.mean(scaled, axis=-1, keepdims=True)
    return (centred - normed * jnp.mean(scaled * normed, axis=-1, keepdims=True)) * inverse


def first_head(shape):
    return lax.broadcasted_iota(jnp.int32, shape, len(shape) - 1) < HD


def attend_kernel(query_ref, key_ref, value_ref, context_ref, log_ref):
    seq_len, width = key_ref.shape
    low = first_head((seq_len, 2 * HD))
    zero = jnp.zeros((), jnp.bfloat16)
    for pair in range(width // (2 * HD)):
        cols = slice(2 * HD * pair, 2 * HD * (pair + 1))
        query, key = query_ref[:, cols], key_ref[:, cols]
        value_t = jnp.transpose(value_ref[:, cols])
        parts = []
        for half in range(2):
            one_key = jnp.where(low if half == 0 else ~low, key, zero)
            scores = dot(one_key, query, NT)
            top = jnp.max(scores, axis=0, keepdims=True)
            weights = jnp.exp2((scores - top) * score_rate)
            total = jnp.sum(weights, axis=0, keepdims=True)
            weights_low = (weights * (1.0 / total)).astype(jnp.bfloat16)
            parts.append(dot(value_t[HD * half : HD * (half + 1)], weights_low))
            head = 2 * pair + half
            log_ref[head : head + 1, :] = top * score_rate + jnp.log2(total)
        context_ref[:, cols] = jnp.transpose(jnp.concatenate(parts, axis=0)).astype(
            context_ref.dtype
        )


def attend(query, key, value):
    rows, width = query.shape
    seq_len = key.shape[0]
    heads = width // HD
    return pl.pallas_call(
        attend_kernel,
        out_shape=(
            jax.ShapeDtypeStruct((rows, width), jnp.bfloat16),
            jax.ShapeDtypeStruct((heads, rows), jnp.float32),
        ),
        compiler_params=pltpu.CompilerParams(vmem_limit_bytes=VMEM_BYTES),
        cost_estimate=pl.CostEstimate(
            flops=16 * rows * seq_len * width,
            bytes_accessed=8 * seq_len * width,
            transcendentals=rows * seq_len * heads,
        ),
        name="attend",
    )(query, key, value)


def attend_back_kernel(
    query_ref, key_ref, value_ref, log_ref, grad_ref, grad_query_ref, grad_key_ref, grad_value_ref
):
    seq_len, width = key_ref.shape
    low = first_head((seq_len, 2 * HD))
    zero = jnp.zeros((), jnp.bfloat16)
    for pair in range(width // (2 * HD)):
        cols = slice(2 * HD * pair, 2 * HD * (pair + 1))
        query, key, value = query_ref[:, cols], key_ref[:, cols], value_ref[:, cols]
        grad = grad_ref[:, cols]
        key_t = jnp.transpose(key)
        grad_query, grad_key, grad_value = [], [], []
        for half in range(2):
            kept = low if half == 0 else ~low
            head = 2 * pair + half
            scores = dot(jnp.where(kept, key, zero), query, NT)
            weights = jnp.exp2(scores * score_rate - log_ref[head : head + 1, :])
            grad_weights = dot(jnp.where(kept, value, zero), grad, NT)
            grad_value.append(dot(weights.astype(jnp.bfloat16), grad))
            row_sum = jnp.sum(grad_weights * weights, axis=0, keepdims=True)
            grad_scores = (weights * (grad_weights - row_sum)).astype(jnp.bfloat16)
            grad_key.append(dot(grad_scores, query))
            grad_query.append(dot(key_t[HD * half : HD * (half + 1)], grad_scores))
        grad_query_ref[:, cols] = (
            jnp.transpose(jnp.concatenate(grad_query, axis=0)) * score_scale
        ).astype(jnp.bfloat16)
        grad_key_ref[:, cols] = (jnp.where(low, grad_key[0], grad_key[1]) * score_scale).astype(
            jnp.bfloat16
        )
        grad_value_ref[:, cols] = jnp.where(low, grad_value[0], grad_value[1]).astype(jnp.bfloat16)


def attend_back(query, key, value, log_total, grad_context):
    seq_len, width = key.shape
    heads = width // HD
    shape = jax.ShapeDtypeStruct((seq_len, width), jnp.bfloat16)
    return pl.pallas_call(
        attend_back_kernel,
        out_shape=(shape, shape, shape),
        compiler_params=pltpu.CompilerParams(vmem_limit_bytes=VMEM_BYTES),
        cost_estimate=pl.CostEstimate(
            flops=40 * seq_len * seq_len * width,
            bytes_accessed=14 * seq_len * width,
            transcendentals=seq_len * seq_len * heads,
        ),
        name="attend_back",
    )(query, key, value, log_total, grad_context)


def make_shards(mesh):
    groups = mesh.shape["dp"]
    bits = groups.bit_length() - 1
    assert groups == 1 << bits and mesh.shape["tensor"] == 2

    def swap_tensor(value):
        return lax.ppermute(value, "tensor", [(0, 1), (1, 0)])

    def swap_bit(value, bit):
        return lax.ppermute(value, "dp", [(i, i ^ (1 << bit)) for i in range(groups)])

    def sum_dp(value):
        for bit in range(bits):
            value = value + swap_bit(value, bit)
        return value

    def own_bit(bit):
        return (lax.axis_index("dp") >> bit) & 1

    def pick(value, which):
        return lax.dynamic_index_in_dim(value, which, axis=1, keepdims=False)

    def scatter_grad(rows_by, columns_by):
        width = rows_by.shape[1]
        part = width // groups
        transposed = rows_by.T.reshape(groups // 2, 2, part, rows_by.shape[0])
        mine = own_bit(0)
        give = dot(pick(transposed, 1 - mine).reshape(width // 2, -1), columns_by)
        keep = dot(pick(transposed, mine).reshape(width // 2, -1), columns_by)
        total = keep + swap_bit(give, 0)
        for bit in range(1, bits):
            split = total.reshape(groups >> (bit + 1), 2, part, -1)
            mine = own_bit(bit)
            total = pick(split, mine) + swap_bit(pick(split, 1 - mine), bit)
        return total.reshape(part, -1)

    def shards(
        images,
        teacher,
        image_mask,
        attn_gain,
        attn_shift,
        in_weight,
        in_bias,
        out_weight,
        out_bias,
        mlp_gain,
        mlp_shift,
        up_weight,
        up_bias,
        down_weight,
        down_bias,
    ):
        image_count, seq_len, width = images.shape
        row_count = image_count * seq_len
        local_width = in_weight.shape[2]
        gain_one = attn_gain.astype(jnp.float32)
        gain_two = mlp_gain.astype(jnp.float32)
        shift_two = mlp_shift.astype(jnp.float32)
        bias_in = in_bias.astype(jnp.float32)
        bias_out = out_bias.astype(jnp.float32)
        bias_up = up_bias.astype(jnp.float32)
        bias_down = down_bias.astype(jnp.float32)
        cut = 256
        chunks = (slice(0, cut), slice(cut, row_count))

        valid = image_mask.astype(jnp.float32)[0]
        count_all = sum_dp(jnp.full((8, 128), valid * seq_len, jnp.float32))[0, 0]

        hidden = images.reshape(row_count, width).astype(jnp.float32)
        targets = teacher.reshape(row_count, width)
        normed_out, normed_one, inverse_one = layer_norm(
            hidden, gain_one, attn_shift.astype(jnp.float32)
        )
        act_one = normed_out.astype(jnp.bfloat16)
        weights_in = jnp.swapaxes(in_weight, 0, 1)
        query = (dot(act_one, weights_in[0]) + bias_in[0]).astype(jnp.bfloat16)
        key = dot(act_one, weights_in[1]).astype(jnp.bfloat16)
        value = (dot(act_one, weights_in[2]) + bias_in[1]).astype(jnp.bfloat16)

        context, log_total, attn_part, middle = [], [], [], []
        for rows in chunks:
            part, logs = attend(query[rows], key, value)
            context.append(part)
            log_total.append(logs)
            attn_part.append(dot(part, out_weight))
        attn_other = [swap_tensor(part) for part in attn_part]
        act_two, inner, slope, mlp_part, normed_two, inverse_two = [], [], [], [], [], []
        for rows, part, other in zip(chunks, attn_part, attn_other):
            mid = hidden[rows] + (part + other) + bias_out
            normed_out, normed, inverse = layer_norm(mid, gain_two, shift_two)
            act = normed_out.astype(jnp.bfloat16)
            pre_act = dot(act, up_weight) + bias_up
            sigma = jax.nn.sigmoid(quick_rate * pre_act)
            low = (pre_act * sigma).astype(jnp.bfloat16)
            middle.append(mid)
            normed_two.append(normed)
            inverse_two.append(inverse)
            act_two.append(act)
            inner.append(low)
            slope.append(sigma + pre_act * quick_rate * sigma * (1.0 - sigma))
            mlp_part.append(dot(low, down_weight))
        mlp_other = [swap_tensor(part) for part in mlp_part]
        result, grad_result, grad_low, grad_pre, two_part = [], [], [], [], []
        squares = jnp.zeros((), jnp.float32)
        for i, rows in enumerate(chunks):
            res = middle[i] + (mlp_part[i] + mlp_other[i]) + bias_down
            error = res - targets[rows].astype(jnp.float32)
            squares = squares + jnp.sum(valid * error * error)
            grad = 2.0 * valid * error / count_all
            low = grad.astype(jnp.bfloat16)
            pre = (dot(low, down_weight, NT) * slope[i]).astype(jnp.bfloat16)
            result.append(res.astype(jnp.bfloat16))
            grad_result.append(grad)
            grad_low.append(low)
            grad_pre.append(pre)
            two_part.append(dot(pre, up_weight, NT))
        two_other = [swap_tensor(part) for part in two_part]
        join = lambda parts: jnp.concatenate(parts, axis=0)
        full_grad_pre = join(grad_pre)
        full_down = scatter_grad(join(grad_low), join(inner))
        full_up = scatter_grad(join(act_two), full_grad_pre)
        grad_down_bias = sum(jnp.sum(part, axis=0) for part in grad_result)
        grad_up_bias = jnp.sum(full_grad_pre.astype(jnp.float32), axis=0)
        grad_middle, grad_attn, grad_context = [], [], []
        grad_mlp_gain = grad_mlp_shift = grad_out_bias = 0.0
        for i, rows in enumerate(chunks):
            grad_two = two_part[i] + two_other[i]
            grad_mlp_gain += jnp.sum(grad_two * normed_two[i], axis=0)
            grad_mlp_shift += jnp.sum(grad_two, axis=0)
            grad_mid = grad_result[i] + norm_back(
                grad_two, normed_two[i], inverse_two[i], gain_two
            )
            grad_out_bias += jnp.sum(grad_mid, axis=0)
            low = grad_mid.astype(jnp.bfloat16)
            grad_middle.append(grad_mid)
            grad_attn.append(low)
            grad_context.append(dot(low, out_weight, NT).astype(jnp.bfloat16))
        full_out = scatter_grad(join(grad_attn), join(context))
        grad_query, grad_key, grad_value = attend_back(
            query, key, value, jnp.concatenate(log_total, axis=1), join(grad_context)
        )
        grad_in_bias = jnp.stack(
            [
                jnp.sum(grad_query.astype(jnp.float32), axis=0),
                jnp.sum(grad_value.astype(jnp.float32), axis=0),
            ]
        )
        one_part = []
        for rows in chunks:
            one_part.append(
                dot(grad_query[rows], weights_in[0], NT)
                + dot(grad_key[rows], weights_in[1], NT)
                + dot(grad_value[rows], weights_in[2], NT)
            )
        one_other = [swap_tensor(part) for part in one_part]
        full_in = scatter_grad(
            act_one, jnp.concatenate([grad_query, grad_key, grad_value], axis=1)
        )
        grad_attn_gain = grad_attn_shift = 0.0
        grad_images = []
        for i, rows in enumerate(chunks):
            grad_attn_gain += jnp.sum(one_part[i] * normed_one[rows], axis=0)
            grad_attn_shift += jnp.sum(one_part[i], axis=0)
            grad_one = one_part[i] + one_other[i]
            grad_images.append(
                (
                    grad_middle[i]
                    + norm_back(grad_one, normed_one[rows], inverse_one[rows], gain_one)
                ).astype(jnp.bfloat16)
            )
        first = jnp.stack([grad_attn_gain, grad_attn_shift])
        first = first + swap_tensor(first)
        small = jnp.concatenate(
            [
                first.reshape(-1),
                grad_in_bias.reshape(-1),
                grad_out_bias,
                grad_mlp_gain,
                grad_mlp_shift,
                grad_up_bias,
                grad_down_bias,
                jnp.full((128,), squares),
            ]
        )
        small = sum_dp(small.reshape(-1, 128)).reshape(-1)
        sizes = (width, width, 2 * local_width, width, width, width, bias_up.shape[0], width, 128)
        pieces = []
        start = 0
        for size in sizes:
            pieces.append(small[start : start + size])
            start += size
        shape = (image_count, seq_len, width)
        return (
            join(result).reshape(shape),
            pieces[8][0] / count_all,
            join(grad_images).reshape(shape),
            pieces[0],
            pieces[1],
            full_in.reshape(-1, 3, local_width),
            pieces[2].reshape(2, local_width),
            full_out.T,
            pieces[3],
            pieces[4],
            pieces[5],
            full_up,
            pieces[6],
            full_down.T,
            pieces[7],
        )

    return shards


def solution(mesh):
    placed = (
        P("dp", None, None),
        P("dp", None, None),
        P("dp"),
        P(),
        P(),
        P(None, None, "tensor"),
        P(None, "tensor"),
        P("tensor", None),
        P(),
        P(),
        P(),
        P(None, "tensor"),
        P("tensor"),
        P("tensor", None),
        P(),
    )
    return jax.shard_map(
        make_shards(mesh),
        mesh=mesh,
        in_specs=placed,
        out_specs=(
            P("dp", None, None),
            P(),
            P("dp", None, None),
            P(),
            P(),
            P("dp", None, "tensor"),
            P(None, "tensor"),
            P("tensor", "dp"),
            P(),
            P(),
            P(),
            P("dp", "tensor"),
            P("tensor"),
            P("tensor", "dp"),
            P(),
        ),
        check_vma=False,
    )
```

time: 790 us -> 491 us (0.62)
  waiting for transfers between devices: 514 us -> 272 us
  blocking collectives: 95.9 us -> 0 us
  starting transfers between devices: 0.97 us -> 39.5 us
  matrix products: 87.8 us -> 60.5 us
  Pallas kernels: 0 us -> 19 us
  other arithmetic: 33.9 us -> 50 us
  between operations: 18.2 us -> 6.64 us
    reduce_scatter x4 -> x0, waiting for transfers between devices: 302 us -> none  [the longest x1 109 us: shards(): lax.psum_scatter(grad_down_weight, 'dp', scatter_dimension=1, tiled=True)]
    ppermute x0 -> x33, waiting for transfers between devices: none -> 272 us  [the longest x24 172 us: swap_bit(): return lax.ppermute(value, 'dp', [(i, i ^ 1 << bit) for i in range(groups)])]
    psum x4 -> x0, waiting for transfers between devices: 212 us -> none  [the longest x1 71.5 us: shards(): attn_branch = lax.psum(attn_part, 'tensor')]
    psum x2 -> x0, blocking collectives: 95.9 us -> none  [shards(): squares_all, count_all = lax.psum((squares_local, count_local), 'dp')]
    ppermute x0 -> x33, starting transfers between devices: none -> 39.5 us  [the longest x24 27.8 us: swap_bit(): return lax.ppermute(value, 'dp', [(i, i ^ 1 << bit) for i in range(groups)])]
    dot_general x18 -> x29, matrix products: 87.8 us -> 60.5 us  [dot(): lax.dot_general(matrix_a, matrix_b, dims, preferred_element_type=jnp.floa...]
    pallas_call x0 -> x3, Pallas kernels: none -> 19 us  [the longest x1 10.1 us: attend_back(): pl.pallas_call(attend_back_kernel, out_shape=(shape, shape, shape), compi...]
    transpose x0 -> x4, local copies, waits for them, and re-layouts: none -> 9.44 us  [scatter_grad(): transposed = rows_by.T.reshape(groups // 2, 2, part, rows_by.shape[0])]
  transfers between devices with their start and end apart: 8 -> 33, of which waited for: 7 -> 19; matrix products, arithmetic and copies ran while one was open for 5% -> 26% of each run, Pallas kernels for 0% -> 3%
where the time goes in v1:
time: 491 us; the launch traced here: 482 us
  waiting for transfers between devices  272 us (55%)
  matrix products  60.5 us (12%)
  other arithmetic  50 us (10%)
  starting transfers between devices  39.5 us (8%)
  local copies, waits for them, and re-layouts  33.8 us (7%)
  Pallas kernels  19 us (4%)
  between operations  6.64 us (1%)
    ppermute x24, waiting for transfers between devices, swap_bit(): return lax.ppermute(value, 'dp', [(i, i ^ 1 << bit) for i in range(groups)])  172 us
    ppermute x9, waiting for transfers between devices, swap_tensor(): return lax.ppermute(value, 'tensor', [(0, 1), (1, 0)])  99.8 us
    dot_general x29, matrix products, dot(): lax.dot_general(matrix_a, matrix_b, dims, preferred_element_type=jnp.floa...  60.5 us
    ppermute x24, starting transfers between devices, swap_bit(): return lax.ppermute(value, 'dp', [(i, i ^ 1 << bit) for i in range(groups)])  27.8 us
    ppermute x9, starting transfers between devices, swap_tensor(): return lax.ppermute(value, 'tensor', [(0, 1), (1, 0)])  11.7 us
    pallas_call x1, Pallas kernels, attend_back(): pl.pallas_call(attend_back_kernel, out_shape=(shape, shape, shape), compi...  10.1 us
  transfers between devices with their start and end apart: 33, of which 19 were waited for; matrix products, arithmetic and copies ran while one was open for 26% of the time, Pallas kernels for 3%

profile of v1, /device:TPU:0, one launch (start us, length us, event | category | flops | bytes accessed | tf_op | source)
XLA Modules:
  0.0 481.8 jit_solution(3633026245985886709)
XLA Ops:
  6.2 2.5 convolution_convert_fusion.key_ref
  10.9 4.5 attend.3
  17.1 2.9 collective-permute-start.2
  21.9 4.5 attend.2
  27.8 2.3 fusion.10
  30.1 2.6 copy.35
  32.7 2.6 constant_dynamic-slice_fusion.11
  42.7 3.0 collective-permute-start.7
  48.2 24.1 %collective-permute-done = f32[256,1024]{1,0:T(8,128)} collective-permute-done((f32[256,1024]{1,0:T(8,128)}, f32[256,1024]{1,0:T(8,128)}, u32[]{:S(2)}, u32[]{:S(2)}) %collective-permute-start) | collective-permute-done | bytes 1048608 | tf_op jit(solution)/shard_map/ppermute | solution.py:141
  72.3 2.2 fusion.36
  75.5 2.9 multiply_convert_fusion.1
  78.4 2.3 fusion.42
  85.1 3.5 multiply_convert_fusion
  88.6 2.7 fusion.44
  92.7 2.8 copy.37
  95.5 11.5 %collective-permute-done.1 = f32[256,1024]{1,0:T(8,128)} collective-permute-done((f32[256,1024]{1,0:T(8,128)}, f32[256,1024]{1,0:T(8,128)}, u32[]{:S(2)}, u32[]{:S(2)}) %collective-permute-start.1) | collective-permute-done | bytes 1048608 | tf_op jit(solution)/shard_map/ppermute | solution.py:141
  107.1 4.0 fusion.11
  112.9 3.5 fusion.1
  116.4 2.4 fusion.45
  120.6 15.3 %collective-permute-done.3 = f32[321,1024]{1,0:T(8,128)} collective-permute-done((f32[321,1024]{1,0:T(8,128)}, f32[321,1024]{1,0:T(8,128)}, u32[]{:S(2)}, u32[]{:S(2)}) %collective-permute-start.3) | collective-permute-done | bytes 1314848 | tf_op jit(solution)/shard_map/ppermute | solution.py:141
  135.9 3.7 fusion.4
  141.8 2.2 fusion
  144.0 2.7 fusion.46
  149.5 2.6 copy.38
  152.1 3.2 constant_dynamic-slice_fusion.2
  155.4 3.7 fusion.16
  159.1 3.8 fusion.3
  166.9 2.3 multiply_reduce_fusion.8
  172.7 12.7 %collective-permute-done.9 = f32[321,1024]{1,0:T(8,128)} collective-permute-done((f32[321,1024]{1,0:T(8,128)}, f32[321,1024]{1,0:T(8,128)}, u32[]{:S(2)}, u32[]{:S(2)}) %collective-permute-start.9) | collective-permute-done | bytes 1314848 | tf_op jit(solution)/shard_map/ppermute | solution.py:141
  185.4 2.5 multiply_reduce_fusion.2
  187.9 2.2 fusion.34
  191.6 10.1 %attend_back.1 = (bf16[577,512]{1,0:T(8,128)(2,1)S(1)}, bf16[577,512]{1,0:T(8,128)(2,1)S(1)}, bf16[577,512]{1,0:T(8,128)(2,1)S(1)}) custom-call(bf16[577,512]{1,0:T(8,128)(2,1)S(1)} %fusion.7.query_ref, bf16[577,512]{1,0:T(8,128)(2,1)S(1)} %convolution_convert_fusion.key_ref, bf16[577,512]{1,0:T(8,128)(2,1)S(1)} %copy-done.4, ...), custom_call_target="tpu_custom_call" | custom-call | flops 6818385920 | bytes 4135936 | tf_op jit(solution)/shard_map/attend_back/pallas_call | solution.py:122
  214.6 3.1 fusion.47
  219.9 11.5 %collective-permute-done.15 = f32[256,1024]{1,0:T(8,128)} collective-permute-done((f32[256,1024]{1,0:T(8,128)}, f32[256,1024]{1,0:T(8,128)}, u32[]{:S(2)}, u32[]{:S(2)}) %collective-permute-start.15) | collective-permute-done | bytes 1048608 | tf_op jit(solution)/shard_map/ppermute | solution.py:141
  234.9 22.5 %collective-permute-done.16 = f32[321,1024]{1,0:T(8,128)S(1)} collective-permute-done((f32[321,1024]{1,0:T(8,128)S(1)}, f32[321,1024]{1,0:T(8,128)S(1)}, u32[]{:S(2)}, u32[]{:S(2)}) %collective-permute-start.16) | collective-permute-done | bytes 1314848 | tf_op jit(solution)/shard_map/ppermute | solution.py:141
  259.4 2.3 collective-permute-done.10
  264.2 2.9 collective-permute-done.12
  268.7 2.5 collective-permute-done.13
  271.2 2.2 collective-permute-start.14
  281.9 4.1 convolution_add_fusion.2
  286.1 3.3 convolution_add_fusion
  293.0 4.1 convolution_add_fusion.1
  299.5 5.7 %collective-permute-done.24 = f32[1,64,512]{2,1,0:T(8,128)S(1)} collective-permute-done((f32[1,64,512]{2,1,0:T(8,128)S(1)}, f32[1,64,512]{2,1,0:T(8,128)S(1)}, u32[]{:S(2)}, u32[]{:S(2)}) %collective-permute-start.24) | collective-permute-done | bytes 131104 | tf_op jit(solution)/shard_map/ppermute | solution.py:144
  305.9 21.1 %collective-permute-done.18 = f32[4,64,1536]{2,1,0:T(8,128)S(1)} collective-permute-done((f32[4,64,1536]{2,1,0:T(8,128)S(1)}, f32[4,64,1536]{2,1,0:T(8,128)S(1)}, u32[]{:S(2)}, u32[]{:S(2)}) %collective-permute-start.18) | collective-permute-done | bytes 1572896 | tf_op jit(solution)/shard_map/ppermute | solution.py:144
  328.9 43.0 %collective-permute-done.26 = f32[4,64,2048]{2,1,0:T(8,128)S(1)} collective-permute-done((f32[4,64,2048]{2,1,0:T(8,128)S(1)}, f32[4,64,2048]{2,1,0:T(8,128)S(1)}, u32[]{:S(2)}, u32[]{:S(2)}) %collective-permute-start.26) | collective-permute-done | bytes 2097184 | tf_op jit(solution)/shard_map/ppermute | solution.py:144
  374.0 38.7 %collective-permute-done.30 = f32[4,64,2048]{2,1,0:T(8,128)S(1)} collective-permute-done((f32[4,64,2048]{2,1,0:T(8,128)S(1)}, f32[4,64,2048]{2,1,0:T(8,128)S(1)}, u32[]{:S(2)}, u32[]{:S(2)}) %collective-permute-start.30) | collective-permute-done | bytes 2097184 | tf_op jit(solution)/shard_map/ppermute | solution.py:144
  418.9 35.0 %collective-permute-done.31 = f32[2,64,2048]{2,1,0:T(8,128)S(1)} collective-permute-done((f32[2,64,2048]{2,1,0:T(8,128)S(1)}, f32[2,64,2048]{2,1,0:T(8,128)S(1)}, u32[]{:S(2)}, u32[]{:S(2)}) %collective-permute-start.31) | collective-permute-done | bytes 1048608 | tf_op jit(solution)/shard_map/ppermute | solution.py:144
  459.8 18.6 %collective-permute-done.32 = f32[1,64,2048]{2,1,0:T(8,128)} collective-permute-done((f32[1,64,2048]{2,1,0:T(8,128)}, f32[1,64,2048]{2,1,0:T(8,128)}, u32[]{:S(2)}, u32[]{:S(2)}) %collective-permute-start.32) | collective-permute-done | bytes 524320 | tf_op jit(solution)/shard_map/ppermute | solution.py:144
  (295 shorter events, 101.1 us)
Async XLA Ops:
  0.6 14.8 %copy-start = (bf16[512,1024]{1,0:T(8,128)(2,1)S(1)}, bf16[512,1024]{1,0:T(8,128)(2,1)}, u32[]{:S(2)}) copy-start(bf16[512,1024]{1,0:T(8,128)(2,1)} %param.22) | copy-start | bytes 3145732
  6.2 41.4 %copy-start.49 = (f32[577]{0:T(1024)}, f32[577]{0:T(1024)S(1)}, u32[]{:S(2)}) copy-start(f32[577]{0:T(1024)S(1)} %add_rsqrt_fusion) | copy-start | bytes 6928
  17.1 65.3 %collective-permute-start.2 = (f32[321,1024]{1,0:T(8,128)}, f32[321,1024]{1,0:T(8,128)}, u32[]{:S(2)}, u32[]{:S(2)}) collective-permute-start(f32[321,1024]{1,0:T(8,128)} %fusion.43), channel_id=1, source_target_pairs={{0,1},{1,0},{2,3},{3,2},{4,5},{5,4},{6,7},{7,6},{8,9},{9,8},{10,11... | collective-permute-start | bytes 3944456 | tf_op jit(solution)/shard_map/ppermute | solution.py:141
  20.7 14.6 %collective-permute-start.4 = (f32[8,128]{1,0:T(8,128)S(1)}, f32[8,128]{1,0:T(8,128)S(1)}, u32[]{:S(2)}, u32[]{:S(2)}) collective-permute-start(f32[8,128]{1,0:T(8,128)S(1)} %broadcast_in_dim.4), channel_id=1, source_target_pairs={{0,2},{2,0},{4,6},{6,4},{8,10},{10,8},{12,14},{14,12},{16,18},{18,... | collective-permute-start | bytes 12296 | tf_op jit(solution)/shard_map/ppermute | solution.py:144
  27.8 44.5 %collective-permute-start = (f32[256,1024]{1,0:T(8,128)}, f32[256,1024]{1,0:T(8,128)}, u32[]{:S(2)}, u32[]{:S(2)}) collective-permute-start(f32[256,1024]{1,0:T(8,128)} %fusion.41), channel_id=1, source_target_pairs={{0,1},{1,0},{2,3},{3,2},{4,5},{5,4},{6,7},{7,6},{8,9},{9,8},{10,11... | collective-permute-start | bytes 3145736 | tf_op jit(solution)/shard_map/ppermute | solution.py:141
  32.7 13.0 %copy-start.11 = (bf16[1,577,1024]{2,1,0:T(8,128)(2,1)S(1)}, bf16[1,577,1024]{2,1,0:T(8,128)(2,1)}, u32[]{:S(2)}) copy-start(bf16[1,577,1024]{2,1,0:T(8,128)(2,1)} %param.15) | copy-start | bytes 3545092
  35.3 3.6 collective-permute-start.5
  39.0 8.6 %copy-start.53 = (bf16[1024]{0:T(1024)(128)(2,1)S(1)}, bf16[1024]{0:T(1024)(128)(2,1)}, u32[]{:S(2)}) copy-start(bf16[1024]{0:T(1024)(128)(2,1)} %param.29) | copy-start | bytes 6148
  39.0 8.6 %copy-start.50 = (bf16[2048]{0:T(1024)(128)(2,1)S(1)}, bf16[2048]{0:T(1024)(128)(2,1)}, u32[]{:S(2)}) copy-start(bf16[2048]{0:T(1024)(128)(2,1)} %param.27) | copy-start | bytes 12292
  39.0 8.6 %copy-start.54 = (bf16[1024]{0:T(1024)(128)(2,1)S(1)}, bf16[1024]{0:T(1024)(128)(2,1)}, u32[]{:S(2)}) copy-start(bf16[1024]{0:T(1024)(128)(2,1)} %param.25) | copy-start | bytes 6148
  39.0 3.7 collective-permute-start.6
  42.7 4.9 %collective-permute-start.7 = (f32[8,128]{1,0:T(8,128)S(1)}, f32[8,128]{1,0:T(8,128)S(1)}, u32[]{:S(2)}, u32[]{:S(2)}) collective-permute-start(f32[8,128]{1,0:T(8,128)S(1)} %add.429), channel_id=1, source_target_pairs={{0,16},{2,18},{4,20},{6,22},{8,24},{10,26},{12,28},{14,30},{16,0},... | collective-permute-start | bytes 12296 | tf_op jit(solution)/shard_map/ppermute | solution.py:144
  80.7 26.4 %collective-permute-start.1 = (f32[256,1024]{1,0:T(8,128)}, f32[256,1024]{1,0:T(8,128)}, u32[]{:S(2)}, u32[]{:S(2)}) collective-permute-start(f32[256,1024]{1,0:T(8,128)} %fusion.42), channel_id=1, source_target_pairs={{0,1},{1,0},{2,3},{3,2},{4,5},{5,4},{6,7},{7,6},{8,9},{9,8},{10,11... | collective-permute-start | bytes 3145736 | tf_op jit(solution)/shard_map/ppermute | solution.py:141
  91.3 44.5 %collective-permute-start.3 = (f32[321,1024]{1,0:T(8,128)}, f32[321,1024]{1,0:T(8,128)}, u32[]{:S(2)}, u32[]{:S(2)}) collective-permute-start(f32[321,1024]{1,0:T(8,128)} %fusion.44), channel_id=1, source_target_pairs={{0,1},{1,0},{2,3},{3,2},{4,5},{5,4},{6,7},{7,6},{8,9},{9,8},{10,11... | collective-permute-start | bytes 3944456 | tf_op jit(solution)/shard_map/ppermute | solution.py:141
  116.4 19.4 %copy-start.6 = (f32[321,1024]{1,0:T(8,128)S(1)}, f32[321,1024]{1,0:T(8,128)}, u32[]{:S(2)}) copy-start(f32[321,1024]{1,0:T(8,128)} %copy-done.5) | copy-start | bytes 3944452
  118.8 48.0 %collective-permute-start.8 = (f32[256,1024]{1,0:T(8,128)}, f32[256,1024]{1,0:T(8,128)}, u32[]{:S(2)}, u32[]{:S(2)}) collective-permute-start(f32[256,1024]{1,0:T(8,128)} %fusion.45), channel_id=1, source_target_pairs={{0,1},{1,0},{2,3},{3,2},{4,5},{5,4},{6,7},{7,6},{8,9},{9,8},{10,11... | collective-permute-start | bytes 3145736 | tf_op jit(solution)/shard_map/ppermute | solution.py:141
  147.8 37.6 %collective-permute-start.9 = (f32[321,1024]{1,0:T(8,128)}, f32[321,1024]{1,0:T(8,128)}, u32[]{:S(2)}, u32[]{:S(2)}) collective-permute-start(f32[321,1024]{1,0:T(8,128)} %fusion.46), channel_id=1, source_target_pairs={{0,1},{1,0},{2,3},{3,2},{4,5},{5,4},{6,7},{7,6},{8,9},{9,8},{10,11... | collective-permute-start | bytes 3944456 | tf_op jit(solution)/shard_map/ppermute | solution.py:141
  159.1 122.8 %collective-permute-start.25 = (f32[512,2048]{1,0:T(8,128)}, f32[512,2048]{1,0:T(8,128)}, u32[]{:S(2)}, u32[]{:S(2)}) collective-permute-start(f32[512,2048]{1,0:T(8,128)} %fusion.16), channel_id=1, source_target_pairs={{0,2},{2,0},{4,6},{6,4},{8,10},{10,8},{12,14},{14,12},{16,18},{18,... | collective-permute-start | bytes 12582920 | tf_op jit(solution)/shard_map/ppermute | solution.py:144
  162.9 129.0 %collective-permute-start.29 = (f32[512,2048]{1,0:T(8,128)}, f32[512,2048]{1,0:T(8,128)}, u32[]{:S(2)}, u32[]{:S(2)}) collective-permute-start(f32[512,2048]{1,0:T(8,128)} %fusion.3), channel_id=1, source_target_pairs={{0,2},{2,0},{4,6},{6,4},{8,10},{10,8},{12,14},{14,12},{16,18},{18,... | collective-permute-start | bytes 12582920 | tf_op jit(solution)/shard_map/ppermute | solution.py:144
  171.2 14.2 %copy-start.7 = (f32[321,1024]{1,0:T(8,128)S(1)}, f32[321,1024]{1,0:T(8,128)}, u32[]{:S(2)}) copy-start(f32[321,1024]{1,0:T(8,128)} %copy-done.5) | copy-start | bytes 3944452
  172.7 15.2 %copy-start.17 = (f32[321,1024]{1,0:T(8,128)S(1)}, f32[321,1024]{1,0:T(8,128)}, u32[]{:S(2)}) copy-start(f32[321,1024]{1,0:T(8,128)} %copy-done.16) | copy-start | bytes 3944452
  191.6 10.1 %copy-start.13 = (bf16[1024,3,512]{2,0,1:T(8,128)(2,1)S(1)}, bf16[1024,3,512]{2,0,1:T(8,128)(2,1)}, u32[]{:S(2)}) copy-start(bf16[1024,3,512]{2,0,1:T(8,128)(2,1)} %param.20) | copy-start | bytes 9437188
  205.0 26.4 %collective-permute-start.15 = (f32[256,1024]{1,0:T(8,128)}, f32[256,1024]{1,0:T(8,128)}, u32[]{:S(2)}, u32[]{:S(2)}) collective-permute-start(f32[256,1024]{1,0:T(8,128)} %convolution_add_fusion.10), channel_id=1, source_target_pairs={{0,1},{1,0},{2,3},{3,2},{4,5},{5,4},{6,7},{7,6},{8,9},{9,8},{10,11... | collective-permute-start | bytes 3145736 | tf_op jit(solution)/shard_map/ppermute | solution.py:141
  211.6 7.2 %collective-permute-start.21 = (f32[512,512]{1,0:T(8,128)S(1)}, f32[512,512]{1,0:T(8,128)S(1)}, u32[]{:S(2)}, u32[]{:S(2)}) collective-permute-start(f32[512,512]{1,0:T(8,128)S(1)} %fusion.48), channel_id=1, source_target_pairs={{0,2},{2,0},{4,6},{6,4},{8,10},{10,8},{12,14},{14,12},{16,18},{18,... | collective-permute-start | bytes 3145736 | tf_op jit(solution)/shard_map/ppermute | solution.py:144
  213.5 43.9 %collective-permute-start.16 = (f32[321,1024]{1,0:T(8,128)S(1)}, f32[321,1024]{1,0:T(8,128)S(1)}, u32[]{:S(2)}, u32[]{:S(2)}) collective-permute-start(f32[321,1024]{1,0:T(8,128)S(1)} %convolution_add_fusion.5), channel_id=1, source_target_pairs={{0,1},{1,0},{2,3},{3,2},{4,5},{5,4},{6,7},{7,6},{8,9},{9,8},{10,11... | collective-permute-start | bytes 3944456 | tf_op jit(solution)/shard_map/ppermute | solution.py:141
  218.8 67.3 %collective-permute-start.17 = (f32[512,1536]{1,0:T(8,128)}, f32[512,1536]{1,0:T(8,128)}, u32[]{:S(2)}, u32[]{:S(2)}) collective-permute-start(f32[512,1536]{1,0:T(8,128)} %fusion.47), channel_id=1, source_target_pairs={{0,2},{2,0},{4,6},{6,4},{8,10},{10,8},{12,14},{14,12},{16,18},{18,... | collective-permute-start | bytes 9437192 | tf_op jit(solution)/shard_map/ppermute | solution.py:144
  219.3 13.6 %copy-start.8 = (f32[577,1024]{1,0:T(8,128)S(1)}, f32[577,1024]{1,0:T(8,128)}, u32[]{:S(2)}) copy-start(f32[577,1024]{1,0:T(8,128)} %get-tuple-element.103) | copy-start | bytes 7090180
  231.4 42.0 %collective-permute-start.22 = (f32[4,64,512]{2,1,0:T(8,128)S(1)}, f32[4,64,512]{2,1,0:T(8,128)S(1)}, u32[]{:S(2)}, u32[]{:S(2)}) collective-permute-start(f32[4,64,512]{2,1,0:T(8,128)S(1)} %dynamic-slice_bitcast_fusion.6), channel_id=1, source_target_pairs={{0,4},{2,6},{4,0},{6,2},{8,12},{10,14},{12,8},{14,10},{16,20},{18,... | collective-permute-start | bytes 1572872 | tf_op jit(solution)/shard_map/ppermute | solution.py:144
  234.9 24.2 %copy-start.22 = (f32[256,1024]{1,0:T(8,128)S(1)}, f32[256,1024]{1,0:T(8,128)}, u32[]{:S(2)}) copy-start(f32[256,1024]{1,0:T(8,128)} %copy-done.21) | copy-start | bytes 3145732
  234.9 24.2 %slice-start = ((f32[577]{0:T(1024)}), f32[256]{0:T(256)S(1)}, s32[]{:S(2)}) async-start(f32[577]{0:T(1024)} %copy-done.49), calls=%async_computation | async-start | bytes 2048 | tf_op jit(solution)/shard_map/slice | solution.py:303
  257.9 10.4 %copy-start.15 = (f32[321,1024]{1,0:T(8,128)S(1)}, f32[321,1024]{1,0:T(8,128)}, u32[]{:S(2)}) copy-start(f32[321,1024]{1,0:T(8,128)} %copy-done.14) | copy-start | bytes 3944452
  258.0 3.7 collective-permute-start.10
  261.8 1.3 collective-permute-start.11
  263.1 4.0 collective-permute-start.12
  267.1 4.1 collective-permute-start.13
  271.2 5.9 %collective-permute-start.14 = (f32[73,128]{1,0:T(8,128)S(1)}, f32[73,128]{1,0:T(8,128)S(1)}, u32[]{:S(2)}, u32[]{:S(2)}) collective-permute-start(f32[73,128]{1,0:T(8,128)S(1)} %add.453), channel_id=1, source_target_pairs={{0,16},{2,18},{4,20},{6,22},{8,24},{10,26},{12,28},{14,30},{16,0},... | collective-permute-start | bytes 112136 | tf_op jit(solution)/shard_map/ppermute | solution.py:144
  274.3 6.5 %collective-permute-start.23 = (f32[2,64,512]{2,1,0:T(8,128)S(1)}, f32[2,64,512]{2,1,0:T(8,128)}, u32[]{:S(2)}, u32[]{:S(2)}) collective-permute-start(f32[2,64,512]{2,1,0:T(8,128)S(1)} %dynamic-slice_bitcast_fusion.7), channel_id=1, source_target_pairs={{0,8},{2,10},{4,12},{6,14},{8,0},{10,2},{12,4},{14,6},{16,24},{18,... | collective-permute-start | bytes 786440 | tf_op jit(solution)/shard_map/ppermute | solution.py:144
  289.6 37.4 %collective-permute-start.18 = (f32[4,64,1536]{2,1,0:T(8,128)S(1)}, f32[4,64,1536]{2,1,0:T(8,128)S(1)}, u32[]{:S(2)}, u32[]{:S(2)}) collective-permute-start(f32[4,64,1536]{2,1,0:T(8,128)S(1)} %dynamic-slice_bitcast_fusion.2), channel_id=1, source_target_pairs={{0,4},{2,6},{4,0},{6,2},{8,12},{10,14},{12,8},{14,10},{16,20},{18,... | collective-permute-start | bytes 4718600 | tf_op jit(solution)/shard_map/ppermute | solution.py:144
  291.4 80.5 %collective-permute-start.26 = (f32[4,64,2048]{2,1,0:T(8,128)S(1)}, f32[4,64,2048]{2,1,0:T(8,128)S(1)}, u32[]{:S(2)}, u32[]{:S(2)}) collective-permute-start(f32[4,64,2048]{2,1,0:T(8,128)S(1)} %dynamic-slice_bitcast_fusion.1), channel_id=1, source_target_pairs={{0,4},{2,6},{4,0},{6,2},{8,12},{10,14},{12,8},{14,10},{16,20},{18,... | collective-permute-start | bytes 6291464 | tf_op jit(solution)/shard_map/ppermute | solution.py:144
  297.3 115.4 %collective-permute-start.30 = (f32[4,64,2048]{2,1,0:T(8,128)S(1)}, f32[4,64,2048]{2,1,0:T(8,128)S(1)}, u32[]{:S(2)}, u32[]{:S(2)}) collective-permute-start(f32[4,64,2048]{2,1,0:T(8,128)S(1)} %dynamic-slice_bitcast_fusion), channel_id=1, source_target_pairs={{0,4},{2,6},{4,0},{6,2},{8,12},{10,14},{12,8},{14,10},{16,20},{18,... | collective-permute-start | bytes 6291464 | tf_op jit(solution)/shard_map/ppermute | solution.py:144
  297.9 7.3 %collective-permute-start.24 = (f32[1,64,512]{2,1,0:T(8,128)S(1)}, f32[1,64,512]{2,1,0:T(8,128)S(1)}, u32[]{:S(2)}, u32[]{:S(2)}) collective-permute-start(f32[1,64,512]{2,1,0:T(8,128)S(1)} %constant_dynamic-slice_fusion.6), channel_id=1, source_target_pairs={{0,16},{2,18},{4,20},{6,22},{8,24},{10,26},{12,28},{14,30},{16,0},... | collective-permute-start | bytes 393224 | tf_op jit(solution)/shard_map/ppermute | solution.py:144
  327.3 87.5 %collective-permute-start.19 = (f32[2,64,1536]{2,1,0:T(8,128)S(1)}, f32[2,64,1536]{2,1,0:T(8,128)S(1)}, u32[]{:S(2)}, u32[]{:S(2)}) collective-permute-start(f32[2,64,1536]{2,1,0:T(8,128)S(1)} %dynamic-slice_bitcast_fusion.5), channel_id=1, source_target_pairs={{0,8},{2,10},{4,12},{6,14},{8,0},{10,2},{12,4},{14,6},{16,24},{18,... | collective-permute-start | bytes 2359304 | tf_op jit(solution)/shard_map/ppermute | solution.py:144
  372.4 43.4 %collective-permute-start.27 = (f32[2,64,2048]{2,1,0:T(8,128)S(1)}, f32[2,64,2048]{2,1,0:T(8,128)S(1)}, u32[]{:S(2)}, u32[]{:S(2)}) collective-permute-start(f32[2,64,2048]{2,1,0:T(8,128)S(1)} %dynamic-slice_bitcast_fusion.4), channel_id=1, source_target_pairs={{0,8},{2,10},{4,12},{6,14},{8,0},{10,2},{12,4},{14,6},{16,24},{18,... | collective-permute-start | bytes 3145736 | tf_op jit(solution)/shard_map/ppermute | solution.py:144
  413.1 40.7 %collective-permute-start.31 = (f32[2,64,2048]{2,1,0:T(8,128)S(1)}, f32[2,64,2048]{2,1,0:T(8,128)S(1)}, u32[]{:S(2)}, u32[]{:S(2)}) collective-permute-start(f32[2,64,2048]{2,1,0:T(8,128)S(1)} %dynamic-slice_bitcast_fusion.3), channel_id=1, source_target_pairs={{0,8},{2,10},{4,12},{6,14},{8,0},{10,2},{12,4},{14,6},{16,24},{18,... | collective-permute-start | bytes 3145736 | tf_op jit(solution)/shard_map/ppermute | solution.py:144
  415.0 39.9 %collective-permute-start.20 = (f32[1,64,1536]{2,1,0:T(8,128)S(1)}, f32[1,64,1536]{2,1,0:T(8,128)S(1)}, u32[]{:S(2)}, u32[]{:S(2)}) collective-permute-start(f32[1,64,1536]{2,1,0:T(8,128)S(1)} %constant_dynamic-slice_fusion.9), channel_id=1, source_target_pairs={{0,16},{2,18},{4,20},{6,22},{8,24},{10,26},{12,28},{14,30},{16,0},... | collective-permute-start | bytes 1179656 | tf_op jit(solution)/shard_map/ppermute | solution.py:144
  416.8 41.2 %collective-permute-start.28 = (f32[1,64,2048]{2,1,0:T(8,128)}, f32[1,64,2048]{2,1,0:T(8,128)}, u32[]{:S(2)}, u32[]{:S(2)}) collective-permute-start(f32[1,64,2048]{2,1,0:T(8,128)} %constant_dynamic-slice_fusion.3), channel_id=1, source_target_pairs={{0,16},{2,18},{4,20},{6,22},{8,24},{10,26},{12,28},{14,30},{16,0},... | collective-permute-start | bytes 1572872 | tf_op jit(solution)/shard_map/ppermute | solution.py:144
  454.9 23.5 %collective-permute-start.32 = (f32[1,64,2048]{2,1,0:T(8,128)}, f32[1,64,2048]{2,1,0:T(8,128)}, u32[]{:S(2)}, u32[]{:S(2)}) collective-permute-start(f32[1,64,2048]{2,1,0:T(8,128)} %constant_dynamic-slice_fusion), channel_id=1, source_target_pairs={{0,16},{2,18},{4,20},{6,22},{8,24},{10,26},{12,28},{14,30},{16,0},... | collective-permute-start | bytes 1572872 | tf_op jit(solution)/shard_map/ppermute | solution.py:144
  454.9 25.4 %copy-start.1 = (bf16[512,1024]{1,0:T(8,128)(2,1)S(1)}, bf16[512,1024]{1,0:T(8,128)(2,1)}, u32[]{:S(2)}) copy-start(bf16[512,1024]{1,0:T(8,128)(2,1)} %param.22) | copy-start | bytes 3145732
  (46 other events, 155.1 us)
